TPU v7x, 32 devices: a whole 2x2x4 slice. The times are simulated.
32 devices in a mesh: sector: 4 (over z), rows: 8 (over y, x, core).
Axes of the slice: x: 2, y: 2, z: 4, core: 2. Of those that a mesh axis runs over, the one named last changes fastest.
Arguments:
- x_block: bfloat16 [4, 10240, 300], P('sector', 'rows')
- h_diag: bfloat16 [4, 10240, 1280], P('sector', 'rows')
- h_right: bfloat16 [4, 10240, 1280], P('sector', 'rows')
- pattern: int32 [4, 2, 80, 10], P('sector', None, 'rows'), may hold values from 0 to 1, as said below
Outputs:
- q_block: bfloat16 [4, 10240, 300], P('sector', 'rows')
- hproj: float32 [4, 300, 300], P('sector')
- correlation: float32 [4, 300, 300], P('sector')
Inputs may be any that keep to these rules, and one draw needn't show every extreme that they name: Within each 1280 x 1280 tile, pattern[s, 0] is symmetric with ones on its diagonal; h_diag's tiles are symmetric.
All inputs are finite; a program needn't handle non-finite values.
Results may differ from a plain program's by a relative error of at most 0.011.
Values may be sent and summed in bfloat16 or wider, within the bound.
No kernel may reach another device: no remote copies, remote signals or barrier semaphores. Data moves between devices by JAX's collectives and lax.ppermute only.
A program may use at most 64 MiB of HBM per device.

v0:
```python
import jax
import jax.numpy as jnp
from jax import lax
from jax.sharding import PartitionSpec as P

SUBBLOCK = 128


def from_behind(value, axis, steps):
    count = lax.axis_size(axis)
    leading, last = (max(0, -steps), min(count, count - steps))
    return lax.ppermute(value, axis, [(source, source + steps) for source in range(leading, last)])


def column_product(left, right):
    return lax.dot_general(
        left, right, (((0,), (0,)), ((), ())), preferred_element_type=jnp.float32
    )


def expand(blocks):
    return jnp.repeat(jnp.repeat(blocks, SUBBLOCK, axis=0), SUBBLOCK, axis=1)


def apply_factor(rows_b, inverse):
    return jnp.dot(rows_b.astype(jnp.float32), inverse.T, precision=lax.Precision.HIGH).astype(
        jnp.bfloat16
    )


def shards(x_block, h_diag, h_right, pattern):
    inputs = x_block[0]
    masks = pattern[0].astype(jnp.bfloat16)
    diag_tile = h_diag[0] * expand(masks[0])
    right_tile = h_right[0] * expand(masks[1])
    later_rows = from_behind(inputs, "rows", -1)
    carried = column_product(right_tile, inputs)
    earlier = from_behind(carried.astype(jnp.bfloat16), "rows", 1).astype(carried.dtype)
    image = jnp.dot(diag_tile, inputs, preferred_element_type=jnp.float32)
    image = image + jnp.dot(right_tile, later_rows, preferred_element_type=jnp.float32) + earlier
    image_b = image.astype(jnp.bfloat16)
    total_rows = lax.axis_size("rows") * inputs.shape[0]
    gram, rayleigh = lax.psum(
        (column_product(image_b, image_b), column_product(inputs, image_b)), "rows"
    )
    gram = gram / total_rows
    rayleigh = rayleigh / total_rows
    factor = jnp.linalg.cholesky(gram)
    inverse = jax.scipy.linalg.solve_triangular(
        factor, jnp.eye(gram.shape[0], dtype=jnp.float32), lower=True
    )
    basis = apply_factor(image_b, inverse)
    previous = from_behind(basis, "sector", 1)
    correlation = (
        lax.psum(column_product(previous, basis).astype(jnp.bfloat16), "rows").astype(jnp.float32)
        / total_rows
    )
    return (basis[None], rayleigh[None], correlation[None])


def solution(mesh):
    in_specs = (
        P("sector", "rows", None),
        P("sector", "rows", None),
        P("sector", "rows", None),
        P("sector", None, "rows", None),
    )
    out_specs = (P("sector", "rows", None), P("sector", None, None), P("sector", None, None))
    return jax.shard_map(shards, mesh=mesh, in_specs=in_specs, out_specs=out_specs, check_vma=False)
```

profile of v0, /device:TPU:0, one launch (start us, length us, event | category | flops | bytes accessed | tf_op | source)
XLA Modules:
  0.0 276.1 jit_solution(8169676560524680616)
XLA Ops:
  8.2 4.0 %copy.16 = bf16[1,1280,1280]{1,2,0:T(8,128)(2,1)S(1)} copy(bf16[1,1280,1280]{2,1,0:T(8,128)(2,1)} %param.6) | data formatting | bytes 6553600 | tf_op args[2]
  12.4 3.2 %fusion.6 = bf16[1280,300]{0,1:T(8,128)(2,1)} fusion(bf16[1,1280,1280]{1,2,0:T(8,128)(2,1)S(1)} %bitcast_multiply_fusion, bf16[1,1280,300]{1,2,0:T(8,128)(2,1)} %param.4), kind=kOutput, calls=%fused_computation.13 | convolution fusion | flops 983424000 | bytes 4812800 | tf_op jit(solution)/shard_map/dot_general | solution.py:16
  15.6 3.2 %collective-permute-start.1 = (bf16[1280,300]{0,1:T(8,128)(2,1)}, bf16[1280,300]{0,1:T(8,128)(2,1)}, u32[]{:S(2)}, u32[]{:S(2)}) collective-permute-start(bf16[1280,300]{0,1:T(8,128)(2,1)} %fusion.6), channel_id=1, source_target_pairs={{0,1},{1,2},{2,3},{3,4},{4,5},{5,6},{6,7},{8,9},{9,10},{10,11},{11... | collective-permute-start | bytes 2304008 | tf_op jit(solution)/shard_map/ppermute | solution.py:12
  18.9 1.3 collective-permute-start
  20.2 1.9 bitcast_multiply_fusion.1
  22.3 4.0 %copy.15 = bf16[1,1280,1280]{1,2,0:T(8,128)(2,1)S(1)} copy(bf16[1,1280,1280]{2,1,0:T(8,128)(2,1)} %param.5) | data formatting | bytes 6553600 | tf_op args[1]
  26.6 2.5 fusion.2
  29.2 2.7 fusion.5
  31.8 2.5 convolution_bitcast_fusion
  34.3 1.4 fusion.39
  36.1 66.6 %all-reduce.9.cloned.1.call-done = (f32[300,300]{0,1:T(8,128)}, f32[300,300]{0,1:T(8,128)}) async-done(((f32[300,300]{0,1:T(8,128)}, f32[300,300]{0,1:T(8,128)}), (f32[300,300]{0,1:T(8,128)}, f32[300,300]{0,1:T(8,128)})) %all-reduce.9.cloned.1.call-update) | async-done | bytes 720016 | tf_op jit(solution)/shard_map/psum | solution.py:43
  105.0 11.7 %cholesky.78 = f32[128,128]{1,0:T(8,128)S(1)} custom-call(f32[128,128]{1,0:T(8,128)S(1)} %cholesky.198), custom_call_target="Cholesky" | custom-call | tf_op jit(solution)/shard_map/jit(cholesky)/cholesky | solution.py:48
  116.8 9.8 %custom-call.23 = f32[1,128,128]{1,2,0:T(8,128)S(1)} custom-call(f32[1,128,128]{2,1,0:T(8,128)S(1)} %get-tuple-element.33), custom_call_target="InvertDiagBlocksLowerTriangular" | custom-call | tf_op jit(solution)/shard_map/jit(cholesky)/cholesky | solution.py:48
  127.2 11.7 %cholesky.164 = f32[128,128]{1,0:T(8,128)S(1)} custom-call(f32[128,128]{1,0:T(8,128)S(1)} %cholesky.202), custom_call_target="Cholesky" | custom-call | tf_op jit(solution)/shard_map/jit(cholesky)/cholesky | solution.py:48
  138.9 10.0 %custom-call.24 = f32[1,128,128]{1,2,0:T(8,128)S(1)} custom-call(f32[1,128,128]{2,1,0:T(8,128)S(1)} %get-tuple-element.30), custom_call_target="InvertDiagBlocksLowerTriangular" | custom-call | tf_op jit(solution)/shard_map/jit(cholesky)/cholesky | solution.py:48
  149.3 4.0 %cholesky.186 = f32[44,44]{1,0:T(8,128)S(1)} custom-call(f32[44,44]{1,0:T(8,128)S(1)} %convolution_subtract_fusion.3), custom_call_target="Cholesky" | custom-call | tf_op jit(solution)/shard_map/jit(cholesky)/cholesky | solution.py:48
  156.7 4.0 %while.1 = (s32[]{:T(128)}, f32[300,300]{1,0:T(8,128)S(1)}, s32[2,2]{1,0:T(2,128)S(1)}, f32[2,128,128]{2,1,0:T(8,128)S(1)}, s32[]{:T(128)}) while((s32[]{:T(128)}, f32[300,300]{1,0:T(8,128)S(1)}, s32[2,2]{1,0:T(2,128)S(1)}, f32[2,128,128]{2,1,0:T(8,128)S(1)}, s32[]{:T(128)}) %tuple.32), condition=%wide.while_cond, body=%wide.while_body.sunk | while | flops 2 | bytes 131181 | solution.py:49
  157.3 1.4 bitcast_dynamic-update-slice_fusion.2
  159.3 1.4 bitcast_dynamic-update-slice_fusion.2
  160.8 29.5 %custom-call.25 = f32[3,128,128]{1,2,0:T(8,128)S(1)} custom-call(f32[3,128,128]{2,1,0:T(8,128)S(1)} %pad_maximum_fusion), custom_call_target="InvertDiagBlocksLowerTriangular" | custom-call | tf_op jit(solution)/shard_map/jit(_solve_triangular)/triangular_solve | solution.py:49
  193.4 3.3 %collective-permute-start.2 = (bf16[1280,300]{0,1:T(8,128)(2,1)S(1)}, bf16[1280,300]{0,1:T(8,128)(2,1)S(1)}, u32[]{:S(2)}, u32[]{:S(2)}) collective-permute-start(bf16[1280,300]{0,1:T(8,128)(2,1)S(1)} %convolution_convert_fusion), channel_id=1, source_target_pairs={{0,8},{8,16},{16,24},{1,9},{9,17},{17,25},{2,10},{10,18},{18,26},{... | collective-permute-start | bytes 2304008 | tf_op jit(solution)/shard_map/ppermute | solution.py:12
  196.7 15.8 %collective-permute-done.2 = bf16[1280,300]{0,1:T(8,128)(2,1)S(1)} collective-permute-done((bf16[1280,300]{0,1:T(8,128)(2,1)S(1)}, bf16[1280,300]{0,1:T(8,128)(2,1)S(1)}, u32[]{:S(2)}, u32[]{:S(2)}) %collective-permute-start.2) | collective-permute-done | bytes 768032 | tf_op jit(solution)/shard_map/ppermute | solution.py:12
  212.5 1.3 convolution_convert_fusion.1
  215.0 52.0 %all-reduce.7.cloned.1.call-done = bf16[300,300]{0,1:T(8,128)(2,1)} async-done(((bf16[300,300]{0,1:T(8,128)(2,1)}), bf16[300,300]{0,1:T(8,128)(2,1)}) %all-reduce.7.cloned.1.call-update) | async-done | bytes 180016 | tf_op jit(solution)/shard_map/psum | solution.py:55
  (64 shorter events, 14.4 us)
Async XLA Ops:
  7.2 95.5 %all-reduce.9.cloned.1.call-start = ((), (), s32[]{:S(2)}) async-start(), calls=%async_computation.1 | async-start | bytes 1867776 | tf_op jit(solution)/shard_map/psum | solution.py:43
  15.6 13.5 %collective-permute-start.1 = (bf16[1280,300]{0,1:T(8,128)(2,1)}, bf16[1280,300]{0,1:T(8,128)(2,1)}, u32[]{:S(2)}, u32[]{:S(2)}) collective-permute-start(bf16[1280,300]{0,1:T(8,128)(2,1)} %fusion.6), channel_id=1, source_target_pairs={{0,1},{1,2},{2,3},{3,4},{4,5},{5,6},{6,7},{8,9},{9,10},{10,11},{11... | collective-permute-start | bytes 2304008 | tf_op jit(solution)/shard_map/ppermute | solution.py:12
  18.9 10.2 %collective-permute-start = (bf16[1280,300]{0,1:T(8,128)(2,1)}, bf16[1280,300]{0,1:T(8,128)(2,1)}, u32[]{:S(2)}, u32[]{:S(2)}) collective-permute-start(bf16[1280,300]{0,1:T(8,128)(2,1)} %bitcast.3), channel_id=1, source_target_pairs={{1,0},{2,1},{3,2},{4,3},{5,4},{6,5},{7,6},{9,8},{10,9},{11,10},{12... | collective-permute-start | bytes 2304008 | tf_op jit(solution)/shard_map/ppermute | solution.py:12
  26.6 2.5 copy-start
  35.7 231.4 %all-reduce.7.cloned.1.call-start = ((), (), s32[]{:S(2)}) async-start(), calls=%async_computation | async-start | bytes 466944 | tf_op jit(solution)/shard_map/psum | solution.py:55
  160.8 53.0 %copy-start.2 = (f32[300,300]{0,1:T(8,128)S(1)}, f32[300,300]{0,1:T(8,128)}, u32[]{:S(2)}) copy-start(f32[300,300]{0,1:T(8,128)} %get-tuple-element.26) | copy-start | bytes 1080004
  193.4 75.9 %copy-start.1 = (bf16[1280,300]{0,1:T(8,128)(2,1)}, bf16[1280,300]{0,1:T(8,128)(2,1)S(1)}, u32[]{:S(2)}) copy-start(bf16[1280,300]{0,1:T(8,128)(2,1)S(1)} %convolution_convert_fusion) | copy-start | bytes 2304004
  193.4 19.1 %collective-permute-start.2 = (bf16[1280,300]{0,1:T(8,128)(2,1)S(1)}, bf16[1280,300]{0,1:T(8,128)(2,1)S(1)}, u32[]{:S(2)}, u32[]{:S(2)}) collective-permute-start(bf16[1280,300]{0,1:T(8,128)(2,1)S(1)} %convolution_convert_fusion), channel_id=1, source_target_pairs={{0,8},{8,16},{16,24},{1,9},{9,17},{17,25},{2,10},{10,18},{18,26},{... | collective-permute-start | bytes 2304008 | tf_op jit(solution)/shard_map/ppermute | solution.py:12
Sparse Core Ops, SparseCore 0:
  35.8 66.7 all-reduce.8
  213.9 53.1 all-reduce.6
where the time goes:
time: 277 us; the launch traced here: 276 us
  waiting for transfers between devices  134 us (48%)
  other arithmetic  84.6 us (31%)
  matrix products  17.4 us (6%)
  between operations  16.4 us (6%)
  local copies, waits for them, and re-layouts  15.1 us (5%)
  starting transfers between devices  8.07 us (3%)
    psum x1, waiting for transfers between devices, shards(): lax.psum((column_product(image_b, image_b), column_product(inputs, image_...  66.6 us
    psum x1, waiting for transfers between devices, shards(): lax.psum(column_product(previous, basis).astype(jnp.bfloat16), 'rows')  52 us
    another operation x10, other arithmetic, shards(): factor = jnp.linalg.cholesky(gram)  48.6 us
    another operation x7, other arithmetic, shards(): jax.scipy.linalg.solve_triangular(factor, jnp.eye(gram.shape[0], dtype=jn...  29.7 us
    ppermute x3, waiting for transfers between devices, from_behind(): lax.ppermute(value, axis, [(source, source + steps) for source in range(l...  15.8 us
    unnamed x16, local copies, waits for them, and re-layouts  10.7 us
    dot_general x4, matrix products, column_product(): lax.dot_general(left, right, (((0,), (0,)), ((), ())), preferred_element_...  8.36 us
    ppermute x3, starting transfers between devices, from_behind(): lax.ppermute(value, axis, [(source, source + steps) for source in range(l...  7.81 us
  transfers between devices with their start and end apart: 5, of which 3 were waited for; matrix products, arithmetic and copies ran while one was open for 4% of the time, Pallas kernels for 0%

commit v1 on v0

v1 whole, which is shorter than its diff:
```python
import functools

import jax
import jax.numpy as jnp
from jax import lax
from jax.experimental import pallas as pl
from jax.experimental.pallas import tpu as pltpu
from jax.sharding import PartitionSpec as P

SUBBLOCK = 128
LANES = 128
PANEL = 16
WHOLE = pl.BlockSpec(memory_space=pltpu.VMEM)
SCALARS = pl.BlockSpec(memory_space=pltpu.SMEM)
ANYWHERE = pl.BlockSpec(memory_space=pl.ANY)
MIB = 1024 * 1024


def params(mib=48):
    return pltpu.CompilerParams(vmem_limit_bytes=mib * MIB)


def cost(flops, bytes_accessed):
    return pl.CostEstimate(flops=flops, bytes_accessed=bytes_accessed, transcendentals=0)


def round_up(value, step):
    return (value + step - 1) // step * step


def dot(left, right, dims, precision=None):
    return lax.dot_general(
        left, right, (dims, ((), ())), precision=precision, preferred_element_type=jnp.float32
    )


def mask_strip(strip_ref, mask_ref, which, row0, col0, rows, cols):
    for i in range(rows // SUBBLOCK):
        for j in range(cols // SUBBLOCK):
            here = (
                slice(row0 + i * SUBBLOCK, row0 + (i + 1) * SUBBLOCK),
                slice(col0 + j * SUBBLOCK, col0 + (j + 1) * SUBBLOCK),
            )
            keep = mask_ref[row0 // SUBBLOCK + i, which, col0 // SUBBLOCK + j]
            strip_ref[here] = strip_ref[here] * keep.astype(strip_ref.dtype)


def strips(rows):
    width = 2 * SUBBLOCK if rows % (2 * SUBBLOCK) == 0 else SUBBLOCK
    return [(start, width) for start in range(0, rows, width)]


def product_kernel(which, mask_ref, x_hbm, tile_hbm, out_ref, x_ref, tile_ref, x_sem, sems):
    rows = tile_ref.shape[0]
    copy_x = pltpu.make_async_copy(x_hbm, x_ref, x_sem)
    copy_x.start()
    copies = []
    for n, (start, width) in enumerate(strips(rows)):
        here = (slice(None), pl.ds(start, width))
        copies.append(pltpu.make_async_copy(tile_hbm.at[here], tile_ref.at[here], sems.at[n]))
        copies[-1].start()
    copy_x.wait()
    for n, (start, width) in enumerate(strips(rows)):
        copies[n].wait()
        mask_strip(tile_ref, mask_ref, which, 0, start, rows, width)
        out_ref[:, start : start + width] = dot(
            x_ref[...], tile_ref[:, start : start + width], ((1,), (0,))
        ).astype(out_ref.dtype)


def tile_product(which, masks, x_t, tile, dtype):
    channels, rows = x_t.shape
    return pl.pallas_call(
        functools.partial(product_kernel, which),
        in_specs=[SCALARS, ANYWHERE, ANYWHERE],
        out_specs=WHOLE,
        out_shape=jax.ShapeDtypeStruct((channels, rows), dtype),
        scratch_shapes=[
            pltpu.VMEM((channels, rows), x_t.dtype),
            pltpu.VMEM((rows, rows), tile.dtype),
            pltpu.SemaphoreType.DMA,
            pltpu.SemaphoreType.DMA((len(strips(rows)),)),
        ],
        compiler_params=params(60),
        cost_estimate=cost(2 * channels * rows * rows, 2 * rows * rows),
    )(masks, x_t, tile)


def later_kernel(mask_ref, x_ref, tile_hbm, first_ref, out_ref, tile_ref, sems):
    rows = tile_ref.shape[0]
    copies = []
    for n, (start, width) in enumerate(strips(rows)):
        here = (pl.ds(start, width), slice(None))
        copies.append(pltpu.make_async_copy(tile_hbm.at[here], tile_ref.at[here], sems.at[n]))
        copies[-1].start()
    for n, (start, width) in enumerate(strips(rows)):
        copies[n].wait()
        mask_strip(tile_ref, mask_ref, 1, start, 0, width, rows)
        here = (slice(None), slice(start, start + width))
        out_ref[here] = first_ref[here] + dot(
            x_ref[...], tile_ref[start : start + width, :], ((1,), (1,))
        )


def later_product(masks, x_t, tile, first):
    channels, rows = x_t.shape
    return pl.pallas_call(
        later_kernel,
        in_specs=[SCALARS, WHOLE, ANYWHERE, WHOLE],
        out_specs=WHOLE,
        out_shape=jax.ShapeDtypeStruct((channels, rows), jnp.float32),
        scratch_shapes=[
            pltpu.VMEM((rows, rows), tile.dtype),
            pltpu.SemaphoreType.DMA((len(strips(rows)),)),
        ],
        compiler_params=params(),
        cost_estimate=cost(2 * channels * rows * rows, 2 * rows * rows),
    )(masks, x_t, tile, first)


def lower_rows(channels):
    rows = round_up(channels, PANEL)
    return sum(rows - g * LANES for g in range(round_up(channels, LANES) // LANES))


def full_rows(channels):
    rows, wide = round_up(channels, PANEL), round_up(channels, LANES)
    whole = channels // LANES
    rest = rows - whole * LANES
    return round_up(whole * rows + rest * (wide // LANES), 4 * PANEL)


def store_padded(ref, value):
    size, tall = value.shape[0], ref.shape[0]
    start = size // PANEL * PANEL
    ref[start:tall, :] = jnp.zeros((tall - start, ref.shape[1]), ref.dtype)
    ref[0:size, :] = value


def lower_products(pad_ref, rows, out_ref):
    offset = 0
    for g in range(pad_ref.shape[0] // LANES):
        block = pad_ref[g * LANES : (g + 1) * LANES, :]
        out_ref[offset : offset + rows - g * LANES, :] = dot(
            pad_ref[g * LANES : rows, :], block, ((1,), (1,))
        )
        offset += rows - g * LANES


def full_products(left_ref, right_ref, channels, out_ref):
    rows, wide = round_up(channels, PANEL), round_up(channels, LANES)
    whole = channels // LANES
    for g in range(whole):
        out_ref[g * rows : (g + 1) * rows, :] = dot(
            left_ref[0:rows, :], right_ref[g * LANES : (g + 1) * LANES, :], ((1,), (1,))
        )
    rest = rows - whole * LANES
    for g in range(wide // LANES if rest else 0):
        out_ref[whole * rows + g * rest : whole * rows + (g + 1) * rest, :] = dot(
            right_ref[whole * LANES : rows, :],
            left_ref[g * LANES : (g + 1) * LANES, :],
            ((1,), (1,)),
        )
    used = whole * rows + rest * (wide // LANES)
    if used < out_ref.shape[0]:
        out_ref[used:, :] = jnp.zeros((out_ref.shape[0] - used, LANES), out_ref.dtype)


def full_matrix(pack_ref, channels):
    rows, wide = round_up(channels, PANEL), round_up(channels, LANES)
    whole = channels // LANES
    rest = rows - whole * LANES
    parts = [pack_ref[g * rows : (g + 1) * rows, :] for g in range(whole)]
    if rest:
        tail = jnp.concatenate(
            [
                pack_ref[whole * rows + g * rest : whole * rows + (g + 1) * rest, :]
                for g in range(wide // LANES)
            ],
            axis=1,
        )
        tail = jnp.concatenate([tail, jnp.zeros((LANES - rest, wide), tail.dtype)], axis=0)
        parts.append(tail.T[0:rows, :])
    return jnp.concatenate(parts, axis=1)


def cut(pack_ref, core, mine_ref, other_ref):
    half = mine_ref.shape[0]
    mine_ref[...] = pack_ref[pl.ds(pl.multiple_of(core * half, 8), half), :].astype(mine_ref.dtype)
    other_ref[...] = pack_ref[pl.ds(pl.multiple_of((1 - core) * half, 8), half), :].astype(
        other_ref.dtype
    )


def join(pack_ref, core, mine, other):
    half = mine.shape[0]
    pack_ref[pl.ds(pl.multiple_of(core * half, 8), half), :] = mine
    pack_ref[pl.ds(pl.multiple_of((1 - core) * half, 8), half), :] = other


def gram_kernel(
    core_ref, part_ref, carried_ref, x_ref, y_ref, g_mine, g_other, r_mine, r_other,
    pad_ref, xpad_ref, gram_ref, ray_ref,
):
    channels = x_ref.shape[0]
    rows = round_up(channels, PANEL)
    image = (part_ref[...] + carried_ref[...].astype(jnp.float32)).astype(y_ref.dtype)
    y_ref[...] = image
    store_padded(pad_ref, image)
    store_padded(xpad_ref, x_ref[...])
    core = core_ref[0]
    lower_products(pad_ref, rows, gram_ref)
    cut(gram_ref, core, g_mine, g_other)
    full_products(xpad_ref, pad_ref, channels, ray_ref)
    cut(ray_ref, core, r_mine, r_other)


def gram(core, part, carried, x_t):
    channels, rows = x_t.shape
    wide = round_up(channels, LANES)
    lower, full = lower_rows(channels), full_rows(channels)
    return pl.pallas_call(
        gram_kernel,
        in_specs=[SCALARS] + [WHOLE] * 3,
        out_specs=[WHOLE] * 5,
        out_shape=[
            jax.ShapeDtypeStruct((channels, rows), x_t.dtype),
            jax.ShapeDtypeStruct((lower // 2, LANES), jnp.float32),
            jax.ShapeDtypeStruct((lower // 2, LANES), jnp.float32),
            jax.ShapeDtypeStruct((full // 2, LANES), jnp.bfloat16),
            jax.ShapeDtypeStruct((full // 2, LANES), jnp.bfloat16),
        ],
        scratch_shapes=[
            pltpu.VMEM((wide, rows), x_t.dtype),
            pltpu.VMEM((wide, rows), x_t.dtype),
            pltpu.VMEM((lower, LANES), jnp.float32),
            pltpu.VMEM((full, LANES), jnp.float32),
        ],
        compiler_params=params(),
        cost_estimate=cost(4 * channels * channels * rows, 8 * channels * rows),
    )(core, part, carried, x_t)


def cross_kernel(core_ref, left_ref, right_ref, after_ref, m_mine, m_other, lpad_ref, pad_ref, pack_ref):
    store_padded(pad_ref, right_ref[...])
    store_padded(lpad_ref, left_ref[...])
    full_products(lpad_ref, pad_ref, left_ref.shape[0], pack_ref)
    cut(pack_ref, core_ref[0], m_mine, m_other)


def cross(core, left, right, after):
    channels, rows = left.shape
    wide, full = round_up(channels, LANES), full_rows(channels)
    return pl.pallas_call(
        cross_kernel,
        in_specs=[SCALARS, WHOLE, WHOLE, ANYWHERE],
        out_specs=[WHOLE] * 2,
        out_shape=[jax.ShapeDtypeStruct((full // 2, LANES), jnp.float32)] * 2,
        scratch_shapes=[
            pltpu.VMEM((wide, rows), left.dtype),
            pltpu.VMEM((wide, rows), left.dtype),
            pltpu.VMEM((full, LANES), jnp.float32),
        ],
        compiler_params=params(),
        cost_estimate=cost(2 * channels * channels * rows, 4 * channels * rows),
    )(core, left, right, after)


def split3(value):
    high = value.astype(jnp.bfloat16)
    rest = value - high.astype(jnp.float32)
    mid = rest.astype(jnp.bfloat16)
    low = (rest - mid.astype(jnp.float32)).astype(jnp.bfloat16)
    return high, mid, low


def sublane(value, index):
    return jnp.broadcast_to(value[index : index + 1, :], value.shape)


def lane_of(value, index):
    return jnp.take_along_axis(value, jnp.broadcast_to(index, value.shape), axis=1)


def eliminate(columns, panel):
    half = 8
    row = lax.broadcasted_iota(jnp.int32, (half, LANES), 0)
    scales = [jnp.zeros((half, LANES), jnp.float32) for _ in range(2)]
    columns = [list(c) for c in columns]
    panel = [list(p) for p in panel]
    for j in range(PANEL):
        h, r = divmod(j, half)
        pivot = sublane(columns[j][h], r)
        inverse = lax.rsqrt(pivot)
        inverse = inverse * (1.5 - 0.5 * pivot * inverse * inverse)
        square = inverse * inverse
        factor = [None, None]
        factor[h] = jnp.where(row > r, columns[j][h], 0.0) * square
        if h == 0:
            factor[1] = columns[j][1] * square
        for later in range(j + 1, PANEL):
            entry = sublane(columns[j][later // half], later % half)
            for t in range(max(h, later // half), 2):
                columns[later][t] = columns[later][t] - factor[t] * entry
        for group in panel:
            entry = sublane(group[h], r)
            for t in range(h, 2):
                group[t] = group[t] - factor[t] * entry
        scales[h] = jnp.where(row == r, inverse, scales[h])
    return [jnp.concatenate([g[0] * scales[0], g[1] * scales[1]], axis=0) for g in panel]


def fill_work(channels, scale, pack_ref, work_ref):
    rows, wide = work_ref.shape
    groups = wide // LANES
    offset = 0
    for g in range(groups):
        top = g * LANES
        size = min(LANES, rows - top)
        column = pack_ref[offset : offset + rows - top, :] * scale
        offset += rows - top
        diag = column[0:size, :]
        if top + LANES > channels:
            row = lax.broadcasted_iota(jnp.int32, diag.shape, 0)
            lane = lax.broadcasted_iota(jnp.int32, diag.shape, 1)
            diag = jnp.where((row == lane) & (lane + top >= channels), 1.0, diag)
        work_ref[top : top + size, top : top + LANES] = diag
        for below in range(g + 1, groups):
            start = (below - g) * LANES
            size_b = min(LANES, rows - below * LANES)
            block = column[start : start + size_b, :]
            if size_b < LANES:
                block = jnp.concatenate(
                    [block, jnp.zeros((LANES - size_b, LANES), jnp.float32)], axis=0
                )
            work_ref[top : top + size, below * LANES : (below + 1) * LANES] = block.T
            work_ref[below * LANES : below * LANES + size_b, top : top + LANES] = jnp.zeros(
                (size_b, LANES), jnp.float32
            )


def eliminate_group(g, work_ref, out_ref):
    rows, wide = work_ref.shape
    groups = wide // LANES
    row = lax.broadcasted_iota(jnp.int32, (PANEL, LANES), 0)
    lane = lax.broadcasted_iota(jnp.int32, (PANEL, LANES), 1)
    top = g * LANES
    size = min(LANES, rows - top)

    def step(b, carry):
        local = b * PANEL
        start = pl.multiple_of(top + local, PANEL)
        place = pl.ds(pl.multiple_of(local, PANEL), PANEL)
        parts = [work_ref[pl.ds(start, PANEL), q * LANES : (q + 1) * LANES] for q in range(groups)]
        pivots = [parts[g][0:8, :], parts[g][8:16, :]]
        columns = [[lane_of(p, local + j) for p in pivots] for j in range(PANEL)]
        inside = (lane >= local) & (lane < local + PANEL)
        identity = jnp.where(lane - local == row, 1.0, 0.0)
        parts[g] = jnp.where(inside, identity, parts[g])
        done = eliminate(columns, [[p[0:8, :], p[8:16, :]] for p in parts])
        left, right = [], []
        for q in range(groups):
            if q < g:
                out_ref[place, q * LANES : (q + 1) * LANES] = done[q]
            elif q == g:
                out_ref[place, q * LANES : (q + 1) * LANES] = jnp.where(
                    lane < local + PANEL, done[q], 0.0
                )
            high, mid, low = split3(done[q])
            right.append(jnp.concatenate([high, mid, high, low, mid, high], axis=0))
            if q >= g:
                if q == g:
                    high, mid, low = split3(jnp.where(lane >= local + PANEL, done[q], 0.0))
                left.append(jnp.concatenate([high, high, mid, high, mid, low], axis=0))
        for n, q in enumerate(range(g, groups)):
            low_row = q * LANES
            high_row = min(rows, low_row + LANES)
            for c in range(groups):
                update = dot(left[n], right[c], ((0,), (0,)))[0 : high_row - low_row, :]
                old = work_ref[low_row:high_row, c * LANES : (c + 1) * LANES]
                if c == g:
                    lanes = lax.broadcasted_iota(jnp.int32, old.shape, 1)
                    old = jnp.where((lanes >= local) & (lanes < local + PANEL), 0.0, old)
                work_ref[low_row:high_row, c * LANES : (c + 1) * LANES] = old - update
        return carry

    lax.fori_loop(0, size // PANEL, step, 0)


def first_stage_kernel(channels, scale, core_ref, mine_ref, other_ref, work_ref, out_ref, pack_ref):
    join(pack_ref, core_ref[0], mine_ref[...], other_ref[...])
    fill_work(channels, scale, pack_ref, work_ref)
    eliminate_group(0, work_ref, out_ref)


def next_stage_kernel(g, before_ref, after_ref, work_ref, out_ref):
    work_ref[...] = before_ref[...]
    eliminate_group(g, work_ref, out_ref)


def stage_shapes(channels, g):
    rows, wide = round_up(channels, PANEL), round_up(channels, LANES)
    return [
        jax.ShapeDtypeStruct((rows, wide), jnp.float32),
        jax.ShapeDtypeStruct((min(LANES, rows - g * LANES), (g + 1) * LANES), jnp.float32),
    ]


def first_stage(core, mine, other, channels, total_rows):
    return pl.pallas_call(
        functools.partial(first_stage_kernel, channels, 1.0 / total_rows),
        in_specs=[SCALARS] + [WHOLE] * 2,
        out_specs=[WHOLE] * 2,
        out_shape=stage_shapes(channels, 0),
        scratch_shapes=[pltpu.VMEM((lower_rows(channels), LANES), jnp.float32)],
        compiler_params=params(),
        cost_estimate=cost(4 * 10**9, 10**6),
    )(core, mine, other)


def next_stage(g, work, channels, after):
    return pl.pallas_call(
        functools.partial(next_stage_kernel, g),
        in_specs=[WHOLE, ANYWHERE],
        out_specs=[WHOLE] * 2,
        out_shape=stage_shapes(channels, g),
        compiler_params=params(),
        cost_estimate=cost(4 * 10**9, 10**6),
    )(work, after)


def split2(value):
    high = value.astype(jnp.bfloat16)
    return high, (value - high.astype(jnp.float32)).astype(jnp.bfloat16)


def dot3(left, right, dims):
    left_high, left_low = split2(left)
    right_high, right_low = split2(right)
    return (
        dot(left_high, right_high, dims)
        + dot(left_high, right_low, dims)
        + dot(left_low, right_high, dims)
    )


def store_inverse(refs, out_ref):
    rows, wide = out_ref.shape
    for g, ref in enumerate(refs):
        top = g * LANES
        out_ref[top : top + ref.shape[0], 0 : ref.shape[1]] = ref[...]
        if ref.shape[1] < wide:
            out_ref[top : top + ref.shape[0], ref.shape[1] : wide] = jnp.zeros(
                (ref.shape[0], wide - ref.shape[1]), jnp.float32
            )


def basis_kernel(*refs):
    y_ref, q_ref, inverse_ref = refs[-3:]
    channels = y_ref.shape[0]
    store_inverse(refs[:-3], inverse_ref)
    high, low = split2(inverse_ref[0:channels, 0:channels])
    image = y_ref[...]
    q_ref[...] = (dot(high, image, ((1,), (0,))) + dot(low, image, ((1,), (0,)))).astype(q_ref.dtype)


def basis(inverse, y_t):
    channels, rows = y_t.shape
    return pl.pallas_call(
        basis_kernel,
        in_specs=[WHOLE] * (len(inverse) + 1),
        out_specs=WHOLE,
        out_shape=jax.ShapeDtypeStruct(y_t.shape, y_t.dtype),
        scratch_shapes=[
            pltpu.VMEM((round_up(channels, PANEL), round_up(channels, LANES)), jnp.float32)
        ],
        compiler_params=params(),
        cost_estimate=cost(4 * channels * channels * rows, 4 * channels * rows),
    )(*inverse, y_t)


def correlation_kernel(scale, core_ref, mine_ref, other_ref, *refs):
    out_ref, pack_ref, inverse_ref, previous_ref = refs[-4:]
    stages = len(refs[:-4]) // 2
    rows = inverse_ref.shape[0]
    channels = out_ref.shape[0]
    store_inverse(refs[:stages], inverse_ref)
    store_inverse(refs[stages : 2 * stages], previous_ref)
    join(pack_ref, core_ref[0], mine_ref[...], other_ref[...])
    half = dot3(full_matrix(pack_ref, channels), inverse_ref[...], ((1,), (1,)))
    total = dot3(previous_ref[:, 0:rows], half, ((1,), (0,))) * scale
    out_ref[...] = total[0:channels, 0:channels]


def correlate(core, mine, other, inverse, previous, channels, total_rows):
    padded = pltpu.VMEM((round_up(channels, PANEL), round_up(channels, LANES)), jnp.float32)
    return pl.pallas_call(
        functools.partial(correlation_kernel, 1.0 / total_rows),
        in_specs=[SCALARS] + [WHOLE] * (2 + 2 * len(inverse)),
        out_specs=WHOLE,
        out_shape=jax.ShapeDtypeStruct((channels, channels), jnp.float32),
        scratch_shapes=[pltpu.VMEM((full_rows(channels), LANES), jnp.float32), padded, padded],
        compiler_params=params(),
        cost_estimate=cost(10**8, 10**6),
    )(core, mine, other, *inverse, *previous)


def unpack_kernel(scale, core_ref, mine_ref, other_ref, out_ref, pack_ref):
    channels = out_ref.shape[0]
    join(pack_ref, core_ref[0], mine_ref[...], other_ref[...])
    out_ref[...] = full_matrix(pack_ref, channels)[0:channels, 0:channels] * scale


def unpack(core, mine, other, channels, total_rows):
    return pl.pallas_call(
        functools.partial(unpack_kernel, 1.0 / total_rows),
        in_specs=[SCALARS] + [WHOLE] * 2,
        out_specs=WHOLE,
        out_shape=jax.ShapeDtypeStruct((channels, channels), jnp.float32),
        scratch_shapes=[pltpu.VMEM((full_rows(channels), LANES), jnp.float32)],
        compiler_params=params(),
        cost_estimate=cost(10**6, 10**6),
    )(core, mine, other)


def from_behind(value, axis, steps):
    count = lax.axis_size(axis)
    leading, last = (max(0, -steps), min(count, count - steps))
    return lax.ppermute(value, axis, [(source, source + steps) for source in range(leading, last)])


def other_core(value):
    return lax.ppermute(value, "rows", [(s, s ^ 1) for s in range(lax.axis_size("rows"))])


def chip_rounds():
    count = lax.axis_size("rows")
    bits = []
    while 2 << len(bits) < count:
        bits.append(2 << len(bits))
    return [
        [(s, s ^ (bits[n] if s % 2 == 0 else bits[-1 - n])) for s in range(count)]
        for n in range(len(bits))
    ]


def sum_half(mine, other):
    kind = mine.dtype
    value = mine.astype(jnp.float32) + other_core(other).astype(jnp.float32)
    for pairs in chip_rounds():
        sent = value.astype(kind)
        value = sent.astype(jnp.float32) + lax.ppermute(sent, "rows", pairs).astype(jnp.float32)
    return value


def shards(x_block, h_diag, h_right, pattern):
    x_t = x_block[0].T
    channels, block_rows = x_t.shape
    masks = pattern[0].transpose(1, 0, 2)
    total_rows = lax.axis_size("rows") * block_rows
    core = (lax.axis_index("rows") % 2).astype(jnp.int32).reshape(1)
    later = from_behind(x_t, "rows", -1)
    carried = from_behind(tile_product(1, masks, x_t, h_right[0], jnp.bfloat16), "rows", 1)
    first = tile_product(0, masks, x_t, h_diag[0], jnp.float32)
    part = later_product(masks, later, h_right[0], first)
    y_t, g_mine, g_other, r_mine, r_other = gram(core, part, carried, x_t)
    previous_y = from_behind(y_t, "sector", 1)
    g_sum = sum_half(g_mine, g_other)
    r_sum = sum_half(r_mine, r_other)
    work, inverse_0 = first_stage(core, g_sum, other_core(g_sum), channels, total_rows)
    inverse = [inverse_0]
    groups = round_up(channels, LANES) // LANES
    after = inverse_0
    for g in range(1, groups):
        if g == groups - 1:
            m_mine, m_other = cross(core, previous_y, y_t, inverse[-1])
            after = m_mine
        work, rows_g = next_stage(g, work, channels, after)
        inverse.append(rows_g)
    m_sum = sum_half(m_mine, m_other)
    previous = [from_behind(rows_g, "sector", 1) for rows_g in inverse]
    q_t = basis(inverse, y_t)
    rayleigh = unpack(core, r_sum, other_core(r_sum), channels, total_rows)
    correlation = correlate(core, m_sum, other_core(m_sum), inverse, previous, channels, total_rows)
    return (q_t.T[None], rayleigh[None], correlation[None])


def solution(mesh):
    in_specs = (
        P("sector", "rows", None),
        P("sector", "rows", None),
        P("sector", "rows", None),
        P("sector", None, "rows", None),
    )
    out_specs = (P("sector", "rows", None), P("sector", None, None), P("sector", None, None))
    return jax.shard_map(shards, mesh=mesh, in_specs=in_specs, out_specs=out_specs, check_vma=False)
```

time: 277 us -> 92.7 us (0.33)
  waiting for transfers between devices: 134 us -> 20.1 us
  other arithmetic: 84.6 us -> 0.2 us
  Pallas kernels: 0 us -> 35.2 us
  starting transfers between devices: 8.07 us -> 32 us
  matrix products: 17.4 us -> 0 us
  between operations: 16.4 us -> 0.9 us
  local copies, waits for them, and re-layouts: 15.1 us -> 3.96 us
    psum x2 -> x0, waiting for transfers between devices: 119 us -> none  [the longest x1 66.6 us: shards(): lax.psum((column_product(image_b, image_b), column_product(inputs, image_...]
    another operation x17 -> x0, other arithmetic: 78.3 us -> none  [the longest x10 48.6 us: shards(): factor = jnp.linalg.cholesky(gram)]
    pallas_call x0 -> x11, Pallas kernels: none -> 35.2 us  [the longest x2 13.3 us: tile_product(): pl.pallas_call(functools.partial(product_kernel, which), in_specs=[SCALAR...]
    dot_general x7 -> x0, matrix products: 14.6 us -> none  [the longest x4 8.36 us: column_product(): lax.dot_general(left, right, (((0,), (0,)), ((), ())), preferred_element_...]
    ppermute x3 -> x6, starting transfers between devices: 7.81 us -> 20.3 us  [from_behind(): lax.ppermute(value, axis, [(source, source + steps) for source in range(l...]
    ppermute x0 -> x12, waiting for transfers between devices: none -> 12.5 us  [the longest x6 11.5 us: sum_half(): lax.ppermute(sent, 'rows', pairs).astype(jnp.float32)]
    ppermute x0 -> x12, starting transfers between devices: none -> 11.6 us  [the longest x6 8.49 us: sum_half(): lax.ppermute(sent, 'rows', pairs).astype(jnp.float32)]
    ppermute x3 -> x6, waiting for transfers between devices: 15.8 us -> 7.58 us  [from_behind(): lax.ppermute(value, axis, [(source, source + steps) for source in range(l...]
  transfers between devices with their start and end apart: 5 -> 18, of which waited for: 3 -> 8; matrix products, arithmetic and copies ran while one was open for 4% -> 2% of each run, Pallas kernels for 0% -> 35%
where the time goes in v1:
time: 92.7 us; the launch traced here: 92.3 us
  Pallas kernels  35.2 us (38%)
  starting transfers between devices  32 us (35%)
  waiting for transfers between devices  20.1 us (22%)
  local copies, waits for them, and re-layouts  3.96 us (4%)
    ppermute x6, starting transfers between devices, from_behind(): lax.ppermute(value, axis, [(source, source + steps) for source in range(l...  20.3 us
    pallas_call x2, Pallas kernels, tile_product(): pl.pallas_call(functools.partial(product_kernel, which), in_specs=[SCALAR...  13.3 us
    ppermute x6, waiting for transfers between devices, sum_half(): lax.ppermute(sent, 'rows', pairs).astype(jnp.float32)  11.5 us
    ppermute x6, starting transfers between devices, sum_half(): lax.ppermute(sent, 'rows', pairs).astype(jnp.float32)  8.49 us
    ppermute x6, waiting for transfers between devices, from_behind(): lax.ppermute(value, axis, [(source, source + steps) for source in range(l...  7.58 us
    pallas_call x2, Pallas kernels, next_stage(): pl.pallas_call(functools.partial(next_stage_kernel, g), in_specs=[WHOLE,...  6.85 us
    pallas_call x1, Pallas kernels, first_stage(): pl.pallas_call(functools.partial(first_stage_kernel, channels, 1.0 / tota...  4.88 us
    pallas_call x1, Pallas kernels, later_product(): pl.pallas_call(later_kernel, in_specs=[SCALARS, WHOLE, ANYWHERE, WHOLE],...  4.73 us
  transfers between devices with their start and end apart: 18, of which 8 were waited for; matrix products, arithmetic and copies ran while one was open for 2% of the time, Pallas kernels for 35%

profile of v1, /device:TPU:0, one launch (start us, length us, event | category | flops | bytes accessed | tf_op | source)
XLA Modules:
  0.0 92.3 jit_solution(11293471846064280208)
XLA Ops:
  0.6 1.3 %collective-permute-start = (bf16[300,1280]{1,0:T(8,128)(2,1)}, bf16[300,1280]{1,0:T(8,128)(2,1)S(1)}, u32[]{:S(2)}, u32[]{:S(2)}) collective-permute-start(bf16[300,1280]{1,0:T(8,128)(2,1)} %bitcast.14), channel_id=1, source_target_pairs={{1,0},{2,1},{3,2},{4,3},{5,4},{6,5},{7,6},{9,8},{10,9},{11,10},{12... | collective-permute-start | bytes 2304008 | tf_op jit(solution)/shard_map/ppermute | solution.py:529
  1.9 6.5 %shard_map.69 = bf16[300,1280]{1,0:T(8,128)(2,1)} custom-call(s32[10,2,10]{2,1,0:T(2,128)} %bitcast.20, bf16[300,1280]{1,0:T(8,128)(2,1)} %bitcast.15, bf16[1280,1280]{1,0:T(8,128)(2,1)} %bitcast.23), custom_call_target="tpu_custom_call" | custom-call | flops 983040000 | bytes 3276800 | tf_op jit(solution)/shard_map/pallas_call | solution.py:73
  8.4 3.1 %collective-permute-start.1 = (bf16[300,1280]{1,0:T(8,128)(2,1)}, bf16[300,1280]{1,0:T(8,128)(2,1)S(1)}, u32[]{:S(2)}, u32[]{:S(2)}) collective-permute-start(bf16[300,1280]{1,0:T(8,128)(2,1)} %shard_map.69), channel_id=1, source_target_pairs={{0,1},{1,2},{2,3},{3,4},{4,5},{5,6},{6,7},{8,9},{9,10},{10,11},{11... | collective-permute-start | bytes 2304008 | tf_op jit(solution)/shard_map/ppermute | solution.py:529
  11.5 6.8 %shard_map.67.first_ref = f32[300,1280]{1,0:T(8,128)} custom-call(s32[10,2,10]{2,1,0:T(2,128)} %bitcast.21, bf16[300,1280]{1,0:T(8,128)(2,1)} %bitcast.16, bf16[1280,1280]{1,0:T(8,128)(2,1)} %bitcast.25), custom_call_target="tpu_custom_call" | custom-call | flops 983040000 | bytes 3276800 | tf_op jit(solution)/shard_map/pallas_call | solution.py:73
  18.4 1.5 %copy-done.1 = f32[300,1280]{1,0:T(8,128)S(1)} copy-done((f32[300,1280]{1,0:T(8,128)S(1)}, f32[300,1280]{1,0:T(8,128)}, u32[]{:S(2)}) %copy-start.1) | copy-done | bytes 1536024
  19.8 4.7 %shard_map.68.part_ref = f32[300,1280]{1,0:T(8,128)S(1)} custom-call(s32[10,2,10]{2,1,0:T(2,128)S(1)} %bitcast.22, bf16[300,1280]{1,0:T(8,128)(2,1)S(1)} %collective-permute-done.x_ref, bf16[1280,1280]{1,0:T(8,128)(2,1)} %bitcast.24, f32[300,1280]{1,0:T(8,128)S(1)} %copy-done.1), custom_call_target="tpu_custom_call" | custom-call | flops 983040000 | bytes 3276800 | tf_op jit(solution)/shard_map/pallas_call | solution.py:107
  24.6 1.3 %shard_map.70 = (bf16[300,1280]{1,0:T(8,128)(2,1)S(1)}, f32[264,128]{1,0:T(8,128)S(1)}, f32[264,128]{1,0:T(8,128)S(1)}, bf16[384,128]{1,0:T(8,128)(2,1)S(1)}, bf16[384,128]{1,0:T(8,128)(2,1)S(1)}) custom-call(s32[1]{0:T(128)} %bitcast.core_ref, f32[300,1280]{1,0:T(8,128)S(1)} %shard_map.68.part_ref, ...), custom_call_target="tpu_custom_call" | custom-call | flops 460800000 | bytes 3072000 | tf_op jit(solution)/shard_map/pallas_call | solution.py:222
  25.9 2.6 %collective-permute-start.2 = (f32[264,128]{1,0:T(8,128)S(1)}, f32[264,128]{1,0:T(8,128)S(1)}, u32[]{:S(2)}, u32[]{:S(2)}) collective-permute-start(f32[264,128]{1,0:T(8,128)S(1)} %get-tuple-element.16), channel_id=1, source_target_pairs={{0,1},{1,0},{2,3},{3,2},{4,5},{5,4},{6,7},{7,6},{8,9},{9,8},{10,11... | collective-permute-start | bytes 405512 | tf_op jit(solution)/shard_map/ppermute | solution.py:533
  29.5 2.4 %collective-permute-start.3 = (f32[264,128]{1,0:T(8,128)S(1)}, f32[264,128]{1,0:T(8,128)S(1)}, u32[]{:S(2)}, u32[]{:S(2)}) collective-permute-start(f32[264,128]{1,0:T(8,128)S(1)} %add.32), channel_id=1, source_target_pairs={{0,2},{1,5},{2,0},{3,7},{4,6},{5,1},{6,4},{7,3},{8,10},{9,13},{10,... | collective-permute-start | bytes 405512 | tf_op jit(solution)/shard_map/ppermute | solution.py:552
  31.9 3.0 %collective-permute-done.3 = f32[264,128]{1,0:T(8,128)S(1)} collective-permute-done((f32[264,128]{1,0:T(8,128)S(1)}, f32[264,128]{1,0:T(8,128)S(1)}, u32[]{:S(2)}, u32[]{:S(2)}) %collective-permute-start.3) | collective-permute-done | bytes 135200 | tf_op jit(solution)/shard_map/ppermute | solution.py:552
  36.2 3.8 %collective-permute-done.4 = f32[264,128]{1,0:T(8,128)S(1)} collective-permute-done((f32[264,128]{1,0:T(8,128)S(1)}, f32[264,128]{1,0:T(8,128)S(1)}, u32[]{:S(2)}, u32[]{:S(2)}) %collective-permute-start.4) | collective-permute-done | bytes 135200 | tf_op jit(solution)/shard_map/ppermute | solution.py:552
  40.1 3.5 %collective-permute-start.6 = (bf16[300,1280]{1,0:T(8,128)(2,1)S(1)}, bf16[300,1280]{1,0:T(8,128)(2,1)S(1)}, u32[]{:S(2)}, u32[]{:S(2)}) collective-permute-start(bf16[300,1280]{1,0:T(8,128)(2,1)S(1)} %get-tuple-element.21.right_ref.refs_3_), channel_id=1, source_target_pairs={{0,8},{8,16},{16,24},{1,9},{9,17},{17,25},{2,10},{10,18},{18,26},{... | collective-permute-start | bytes 2304008 | tf_op jit(solution)/shard_map/ppermute | solution.py:529
  43.9 4.9 %shard_map.71 = (f32[304,384]{1,0:T(8,128)S(1)}, f32[128,128]{1,0:T(8,128)S(1)}) custom-call(s32[1]{0:T(128)} %bitcast.core_ref, f32[264,128]{1,0:T(8,128)S(1)} %add.34.mine_ref, f32[264,128]{1,0:T(8,128)S(1)} %collective-permute-done.5.other_ref), custom_call_target="tpu_custom_call" | custom-call | flops 4000000000 | bytes 1000000 | tf_op jit(solution)/shard_map/pallas_call | solution.py:410
  48.8 4.5 %shard_map.72 = (f32[304,384]{1,0:T(8,128)S(1)}, f32[128,256]{1,0:T(8,128)S(1)}) custom-call(f32[304,384]{1,0:T(8,128)S(1)} %get-tuple-element.18.before_ref, f32[128,128]{1,0:T(8,128)S(1)} %get-tuple-element.17.after_ref.refs_0_), custom_call_target="tpu_custom_call" | custom-call | flops 4000000000 | bytes 1000000 | tf_op jit(solution)/shard_map/pallas_call | solution.py:422
  53.3 7.6 %collective-permute-done.6.left_ref = bf16[300,1280]{1,0:T(8,128)(2,1)S(1)} collective-permute-done((bf16[300,1280]{1,0:T(8,128)(2,1)S(1)}, bf16[300,1280]{1,0:T(8,128)(2,1)S(1)}, u32[]{:S(2)}, u32[]{:S(2)}) %collective-permute-start.6) | collective-permute-done | bytes 768032 | tf_op jit(solution)/shard_map/ppermute | solution.py:529
  61.8 2.1 %collective-permute-start.8 = (bf16[384,128]{1,0:T(8,128)(2,1)S(1)}, bf16[384,128]{1,0:T(8,128)(2,1)S(1)}, u32[]{:S(2)}, u32[]{:S(2)}) collective-permute-start(bf16[384,128]{1,0:T(8,128)(2,1)S(1)} %add_convert_fusion.1), channel_id=1, source_target_pairs={{0,2},{1,5},{2,0},{3,7},{4,6},{5,1},{6,4},{7,3},{8,10},{9,13},{10,... | collective-permute-start | bytes 294920 | tf_op jit(solution)/shard_map/ppermute | solution.py:552
  64.0 1.4 %collective-permute-start.12 = (f32[384,128]{1,0:T(8,128)S(1)}, f32[384,128]{1,0:T(8,128)S(1)}, u32[]{:S(2)}, u32[]{:S(2)}) collective-permute-start(f32[384,128]{1,0:T(8,128)S(1)} %add.38), channel_id=1, source_target_pairs={{0,2},{1,5},{2,0},{3,7},{4,6},{5,1},{6,4},{7,3},{8,10},{9,13},{10,... | collective-permute-start | bytes 589832 | tf_op jit(solution)/shard_map/ppermute | solution.py:552
  67.8 2.4 %collective-permute-done.12 = f32[384,128]{1,0:T(8,128)S(1)} collective-permute-done((f32[384,128]{1,0:T(8,128)S(1)}, f32[384,128]{1,0:T(8,128)S(1)}, u32[]{:S(2)}, u32[]{:S(2)}) %collective-permute-start.12) | collective-permute-done | bytes 196640 | tf_op jit(solution)/shard_map/ppermute | solution.py:552
  71.3 4.4 %collective-permute-start.16 = (f32[128,256]{1,0:T(8,128)S(1)}, f32[128,256]{1,0:T(8,128)S(1)}, u32[]{:S(2)}, u32[]{:S(2)}) collective-permute-start(f32[128,256]{1,0:T(8,128)S(1)} %get-tuple-element.19.after_ref.refs_1_), channel_id=1, source_target_pairs={{0,8},{8,16},{16,24},{1,9},{9,17},{17,25},{2,10},{10,18},{18,26},{... | collective-permute-start | bytes 393224 | tf_op jit(solution)/shard_map/ppermute | solution.py:529
  76.1 2.4 %shard_map.74 = (f32[304,384]{1,0:T(8,128)}, f32[48,384]{1,0:T(8,128)S(1)}) custom-call(f32[304,384]{1,0:T(8,128)S(1)} %get-tuple-element.20.before_ref, f32[384,128]{1,0:T(8,128)S(1)} %get-tuple-element.22.after_ref), custom_call_target="tpu_custom_call" | custom-call | flops 4000000000 | bytes 1000000 | tf_op jit(solution)/shard_map/pallas_call | solution.py:422
  78.4 4.4 %collective-permute-start.17 = (f32[48,384]{1,0:T(8,128)S(1)}, f32[48,384]{1,0:T(8,128)S(1)}, u32[]{:S(2)}, u32[]{:S(2)}) collective-permute-start(f32[48,384]{1,0:T(8,128)S(1)} %get-tuple-element.23.refs_2_), channel_id=1, source_target_pairs={{0,8},{8,16},{16,24},{1,9},{9,17},{17,25},{2,10},{10,18},{18,26},{... | collective-permute-start | bytes 221192 | tf_op jit(solution)/shard_map/ppermute | solution.py:529
  82.8 3.7 %collective-permute-start.15 = (f32[128,128]{1,0:T(8,128)S(1)}, f32[128,128]{1,0:T(8,128)S(1)}, u32[]{:S(2)}, u32[]{:S(2)}) collective-permute-start(f32[128,128]{1,0:T(8,128)S(1)} %get-tuple-element.17.after_ref.refs_0_), channel_id=1, source_target_pairs={{0,8},{8,16},{16,24},{1,9},{9,17},{17,25},{2,10},{10,18},{18,26},{... | collective-permute-start | bytes 196616 | tf_op jit(solution)/shard_map/ppermute | solution.py:529
  87.9 1.8 %shard_map.75 = bf16[300,1280]{1,0:T(8,128)(2,1)} custom-call(f32[128,128]{1,0:T(8,128)S(1)} %get-tuple-element.17.after_ref.refs_0_, f32[128,256]{1,0:T(8,128)S(1)} %get-tuple-element.19.after_ref.refs_1_, f32[48,384]{1,0:T(8,128)S(1)} %get-tuple-element.23.refs_2_, bf16[300,1280]{1,0:T(8,128)(2,1)S(1)} %get-tuple-element.21.right_ref.refs_3_), custom_call_target="tpu_custom_call" | custom-call | flops 460800000 | bytes 1536000 | tf_op jit(solution)/shard_map/pallas_call | solution.py:469
  89.8 1.3 %shard_map.77 = f32[300,300]{1,0:T(8,128)S(1)} custom-call(s32[1]{0:T(128)} %bitcast.core_ref, f32[384,128]{1,0:T(8,128)S(1)} %add.40.mine_ref, f32[384,128]{1,0:T(8,128)S(1)} %collective-permute-done.14.other_ref, f32[128,128]{1,0:T(8,128)S(1)} %get-tuple-element.17.after_ref.refs_0_, f32[128,256]{1,0:T(8,128)S(1)} %get-tuple-element.19.after_ref.refs_1_, ...), custom_call_target="tpu_custom_call" | custom-call | flops 100000000 | bytes 1000000 | tf_op jit(solution)/shard_map/pallas_call | solution.py:497
  (40 shorter events, 10.2 us)
Async XLA Ops:
  0.6 17.7 %collective-permute-start = (bf16[300,1280]{1,0:T(8,128)(2,1)}, bf16[300,1280]{1,0:T(8,128)(2,1)S(1)}, u32[]{:S(2)}, u32[]{:S(2)}) collective-permute-start(bf16[300,1280]{1,0:T(8,128)(2,1)} %bitcast.14), channel_id=1, source_target_pairs={{1,0},{2,1},{3,2},{4,3},{5,4},{6,5},{7,6},{9,8},{10,9},{11,10},{12... | collective-permute-start | bytes 2304008 | tf_op jit(solution)/shard_map/ppermute | solution.py:529
  8.4 9.9 %copy-start.2 = (s32[1,2,10,10]{3,1,2,0:T(2,128)S(1)}, s32[1,2,10,10]{3,1,2,0:T(2,128)}, u32[]{:S(2)}) copy-start(s32[1,2,10,10]{3,1,2,0:T(2,128)} %param.7) | copy-start | bytes 2404
  8.4 16.1 %collective-permute-start.1 = (bf16[300,1280]{1,0:T(8,128)(2,1)}, bf16[300,1280]{1,0:T(8,128)(2,1)S(1)}, u32[]{:S(2)}, u32[]{:S(2)}) collective-permute-start(bf16[300,1280]{1,0:T(8,128)(2,1)} %shard_map.69), channel_id=1, source_target_pairs={{0,1},{1,2},{2,3},{3,4},{4,5},{5,6},{6,7},{8,9},{9,10},{10,11},{11... | collective-permute-start | bytes 2304008 | tf_op jit(solution)/shard_map/ppermute | solution.py:529
  18.3 6.3 %copy-start = (bf16[1,1280,300]{1,2,0:T(8,128)(2,1)S(1)}, bf16[1,1280,300]{1,2,0:T(8,128)(2,1)}, u32[]{:S(2)}) copy-start(bf16[1,1280,300]{1,2,0:T(8,128)(2,1)} %param.4) | copy-start | bytes 2304004
  18.4 1.5 %copy-start.1 = (f32[300,1280]{1,0:T(8,128)S(1)}, f32[300,1280]{1,0:T(8,128)}, u32[]{:S(2)}) copy-start(f32[300,1280]{1,0:T(8,128)} %shard_map.67.first_ref) | copy-start | bytes 4608004
  25.9 3.6 %collective-permute-start.2 = (f32[264,128]{1,0:T(8,128)S(1)}, f32[264,128]{1,0:T(8,128)S(1)}, u32[]{:S(2)}, u32[]{:S(2)}) collective-permute-start(f32[264,128]{1,0:T(8,128)S(1)} %get-tuple-element.16), channel_id=1, source_target_pairs={{0,1},{1,0},{2,3},{3,2},{4,5},{5,4},{6,7},{7,6},{8,9},{9,8},{10,11... | collective-permute-start | bytes 405512 | tf_op jit(solution)/shard_map/ppermute | solution.py:533
  29.5 5.4 %collective-permute-start.3 = (f32[264,128]{1,0:T(8,128)S(1)}, f32[264,128]{1,0:T(8,128)S(1)}, u32[]{:S(2)}, u32[]{:S(2)}) collective-permute-start(f32[264,128]{1,0:T(8,128)S(1)} %add.32), channel_id=1, source_target_pairs={{0,2},{1,5},{2,0},{3,7},{4,6},{5,1},{6,4},{7,3},{8,10},{9,13},{10,... | collective-permute-start | bytes 405512 | tf_op jit(solution)/shard_map/ppermute | solution.py:552
  34.9 5.1 %collective-permute-start.4 = (f32[264,128]{1,0:T(8,128)S(1)}, f32[264,128]{1,0:T(8,128)S(1)}, u32[]{:S(2)}, u32[]{:S(2)}) collective-permute-start(f32[264,128]{1,0:T(8,128)S(1)} %add.33), channel_id=1, source_target_pairs={{0,4},{1,3},{2,6},{3,1},{4,0},{5,7},{6,2},{7,5},{8,12},{9,11},{10,... | collective-permute-start | bytes 405512 | tf_op jit(solution)/shard_map/ppermute | solution.py:552
  40.0 3.9 %collective-permute-start.5 = (f32[264,128]{1,0:T(8,128)S(1)}, f32[264,128]{1,0:T(8,128)S(1)}, u32[]{:S(2)}, u32[]{:S(2)}) collective-permute-start(f32[264,128]{1,0:T(8,128)S(1)} %add.34.mine_ref), channel_id=1, source_target_pairs={{0,1},{1,0},{2,3},{3,2},{4,5},{5,4},{6,7},{7,6},{8,9},{9,8},{10,11... | collective-permute-start | bytes 405512 | tf_op jit(solution)/shard_map/ppermute | solution.py:533
  40.1 20.7 %collective-permute-start.6 = (bf16[300,1280]{1,0:T(8,128)(2,1)S(1)}, bf16[300,1280]{1,0:T(8,128)(2,1)S(1)}, u32[]{:S(2)}, u32[]{:S(2)}) collective-permute-start(bf16[300,1280]{1,0:T(8,128)(2,1)S(1)} %get-tuple-element.21.right_ref.refs_3_), channel_id=1, source_target_pairs={{0,8},{8,16},{16,24},{1,9},{9,17},{17,25},{2,10},{10,18},{18,26},{... | collective-permute-start | bytes 2304008 | tf_op jit(solution)/shard_map/ppermute | solution.py:529
  43.6 18.2 %collective-permute-start.7 = (bf16[384,128]{1,0:T(8,128)(2,1)S(1)}, bf16[384,128]{1,0:T(8,128)(2,1)S(1)}, u32[]{:S(2)}, u32[]{:S(2)}) collective-permute-start(bf16[384,128]{1,0:T(8,128)(2,1)S(1)} %get-tuple-element.25), channel_id=1, source_target_pairs={{0,1},{1,0},{2,3},{3,2},{4,5},{5,4},{6,7},{7,6},{8,9},{9,8},{10,11... | collective-permute-start | bytes 294920 | tf_op jit(solution)/shard_map/ppermute | solution.py:533
  61.7 2.2 %collective-permute-start.11 = (f32[384,128]{1,0:T(8,128)S(1)}, f32[384,128]{1,0:T(8,128)S(1)}, u32[]{:S(2)}, u32[]{:S(2)}) collective-permute-start(f32[384,128]{1,0:T(8,128)S(1)} %get-tuple-element.26), channel_id=1, source_target_pairs={{0,1},{1,0},{2,3},{3,2},{4,5},{5,4},{6,7},{7,6},{8,9},{9,8},{10,11... | collective-permute-start | bytes 589832 | tf_op jit(solution)/shard_map/ppermute | solution.py:533
  61.8 4.7 %collective-permute-start.8 = (bf16[384,128]{1,0:T(8,128)(2,1)S(1)}, bf16[384,128]{1,0:T(8,128)(2,1)S(1)}, u32[]{:S(2)}, u32[]{:S(2)}) collective-permute-start(bf16[384,128]{1,0:T(8,128)(2,1)S(1)} %add_convert_fusion.1), channel_id=1, source_target_pairs={{0,2},{1,5},{2,0},{3,7},{4,6},{5,1},{6,4},{7,3},{8,10},{9,13},{10,... | collective-permute-start | bytes 294920 | tf_op jit(solution)/shard_map/ppermute | solution.py:552
  64.0 6.2 %collective-permute-start.12 = (f32[384,128]{1,0:T(8,128)S(1)}, f32[384,128]{1,0:T(8,128)S(1)}, u32[]{:S(2)}, u32[]{:S(2)}) collective-permute-start(f32[384,128]{1,0:T(8,128)S(1)} %add.38), channel_id=1, source_target_pairs={{0,2},{1,5},{2,0},{3,7},{4,6},{5,1},{6,4},{7,3},{8,10},{9,13},{10,... | collective-permute-start | bytes 589832 | tf_op jit(solution)/shard_map/ppermute | solution.py:552
  66.6 4.7 %collective-permute-start.9 = (bf16[384,128]{1,0:T(8,128)(2,1)S(1)}, bf16[384,128]{1,0:T(8,128)(2,1)S(1)}, u32[]{:S(2)}, u32[]{:S(2)}) collective-permute-start(bf16[384,128]{1,0:T(8,128)(2,1)S(1)} %add_convert_fusion), channel_id=1, source_target_pairs={{0,4},{1,3},{2,6},{3,1},{4,0},{5,7},{6,2},{7,5},{8,12},{9,11},{10,... | collective-permute-start | bytes 294920 | tf_op jit(solution)/shard_map/ppermute | solution.py:552
  70.2 5.7 %collective-permute-start.13 = (f32[384,128]{1,0:T(8,128)S(1)}, f32[384,128]{1,0:T(8,128)S(1)}, u32[]{:S(2)}, u32[]{:S(2)}) collective-permute-start(f32[384,128]{1,0:T(8,128)S(1)} %add.39), channel_id=1, source_target_pairs={{0,4},{1,3},{2,6},{3,1},{4,0},{5,7},{6,2},{7,5},{8,12},{9,11},{10,... | collective-permute-start | bytes 589832 | tf_op jit(solution)/shard_map/ppermute | solution.py:552
  71.3 15.2 %collective-permute-start.10 = (f32[384,128]{1,0:T(8,128)S(1)}, f32[384,128]{1,0:T(8,128)S(1)}, u32[]{:S(2)}, u32[]{:S(2)}) collective-permute-start(f32[384,128]{1,0:T(8,128)S(1)} %convert_add_fusion.mine_ref), channel_id=1, source_target_pairs={{0,1},{1,0},{2,3},{3,2},{4,5},{5,4},{6,7},{7,6},{8,9},{9,8},{10,11... | collective-permute-start | bytes 589832 | tf_op jit(solution)/shard_map/ppermute | solution.py:533
  71.3 18.4 %collective-permute-start.16 = (f32[128,256]{1,0:T(8,128)S(1)}, f32[128,256]{1,0:T(8,128)S(1)}, u32[]{:S(2)}, u32[]{:S(2)}) collective-permute-start(f32[128,256]{1,0:T(8,128)S(1)} %get-tuple-element.19.after_ref.refs_1_), channel_id=1, source_target_pairs={{0,8},{8,16},{16,24},{1,9},{9,17},{17,25},{2,10},{10,18},{18,26},{... | collective-permute-start | bytes 393224 | tf_op jit(solution)/shard_map/ppermute | solution.py:529
  76.0 13.8 %collective-permute-start.14 = (f32[384,128]{1,0:T(8,128)S(1)}, f32[384,128]{1,0:T(8,128)S(1)}, u32[]{:S(2)}, u32[]{:S(2)}) collective-permute-start(f32[384,128]{1,0:T(8,128)S(1)} %add.40.mine_ref), channel_id=1, source_target_pairs={{0,1},{1,0},{2,3},{3,2},{4,5},{5,4},{6,7},{7,6},{8,9},{9,8},{10,11... | collective-permute-start | bytes 589832 | tf_op jit(solution)/shard_map/ppermute | solution.py:533
  78.4 11.3 %collective-permute-start.17 = (f32[48,384]{1,0:T(8,128)S(1)}, f32[48,384]{1,0:T(8,128)S(1)}, u32[]{:S(2)}, u32[]{:S(2)}) collective-permute-start(f32[48,384]{1,0:T(8,128)S(1)} %get-tuple-element.23.refs_2_), channel_id=1, source_target_pairs={{0,8},{8,16},{16,24},{1,9},{9,17},{17,25},{2,10},{10,18},{18,26},{... | collective-permute-start | bytes 221192 | tf_op jit(solution)/shard_map/ppermute | solution.py:529
  82.8 6.9 %collective-permute-start.15 = (f32[128,128]{1,0:T(8,128)S(1)}, f32[128,128]{1,0:T(8,128)S(1)}, u32[]{:S(2)}, u32[]{:S(2)}) collective-permute-start(f32[128,128]{1,0:T(8,128)S(1)} %get-tuple-element.17.after_ref.refs_0_), channel_id=1, source_target_pairs={{0,8},{8,16},{16,24},{1,9},{9,17},{17,25},{2,10},{10,18},{18,26},{... | collective-permute-start | bytes 196616 | tf_op jit(solution)/shard_map/ppermute | solution.py:529
